TPU v7x, 32 devices: a whole 2x2x4 slice. The times are simulated.
32 devices in a mesh: grp: 2 (over y), row: 4 (over z), col: 2 (over x), freq: 2 (over core).
Axes of the slice: x: 2, y: 2, z: 4, core: 2. Of those that a mesh axis runs over, the one named last changes fastest.
Arguments:
- w_freq: bfloat16 [64, 288, 4096], P(('grp', 'freq'), 'row', 'col'), parts along dimension 0, may hold values from -6 to 6
- x_rows: bfloat16 [576, 2048], P(('grp', 'row')), parts along dimension 0, may hold values from -6 to 6
- x_cols: bfloat16 [8192, 2048], P(('grp', 'col', 'freq')), parts along dimension 0, may hold values from -6 to 6
- occupation: float32 [8, 2048], P('grp'), parts along dimension 0, may hold values from 0.05 to 1
Outputs:
- sigma_orb: float32 [8, 2048, 2048], P('grp', 'row', ('col', 'freq')), parts along dimension 0
There are 2 independent parts, one for each index of `grp`. A program takes and returns all parts, laid end to end along the dimension named above; each array names one. Nothing has to cross between parts.
All inputs are finite; a program needn't handle non-finite values.
Results may differ from a plain program's by a relative error of at most 0.005.
Values may be sent and summed in bfloat16 or wider, within the bound.
A program may use at most 128 MiB of HBM per device.

v0:
```python
import math

import jax
import jax.numpy as jnp
from jax import lax
from jax.sharding import PartitionSpec as P


def bosonic_table(tau_count, freq_count):
    omega = jnp.arange(freq_count, dtype=jnp.float32)
    steps_tau = jnp.arange(tau_count, dtype=jnp.float32) + 1.0
    weights = jnp.where(omega == 0.0, 1.0, 2.0).astype(jnp.float32)
    phases = 2.0 * math.pi * steps_tau[:, None] * omega[None, :] / (tau_count + 1.0)
    return weights[None, :] * jnp.cos(phases) / math.sqrt(2.0 * freq_count)


def local(w_freq, x_rows, x_cols, occupation):
    local_freq, rows_dev, cols_dev = w_freq.shape
    freq_count = local_freq * lax.axis_size("freq")
    tau_count = occupation.shape[0]
    norb_count = x_rows.shape[1]
    point_count = x_cols.shape[0] * lax.axis_size("col") * lax.axis_size("freq")
    transform = bosonic_table(tau_count, freq_count)
    regrouped = lax.all_to_all(w_freq, "freq", split_axis=2, concat_axis=0, tiled=True)
    flattened = regrouped.reshape(freq_count, -1).astype(jnp.float32)
    w_tau = jnp.dot(transform, flattened, precision=lax.Precision.HIGHEST).reshape(
        tau_count, rows_dev, -1
    )
    scaled = (x_rows.astype(jnp.float32)[None, :, :] * occupation[:, None, :]).astype(jnp.bfloat16)
    green_tau = jnp.einsum(
        "tpk,qk->tpq", scaled, x_cols, preferred_element_type=jnp.float32
    ) / math.sqrt(norb_count)
    sigma_tau = (green_tau * w_tau).astype(jnp.bfloat16)
    half_terms = jnp.einsum(
        "tpq,qj->tpj", sigma_tau, x_cols, preferred_element_type=jnp.float32
    ) / math.sqrt(point_count)
    half_proj = lax.psum_scatter(
        half_terms, ("col", "freq"), scatter_dimension=2, tiled=True
    ).astype(jnp.bfloat16)
    row_basis = lax.all_to_all(x_rows, "row", split_axis=1, concat_axis=0, tiled=True)
    rows_total = row_basis.shape[0]
    running = jnp.einsum(
        "pi,tpj->tij",
        row_basis,
        lax.all_gather(half_proj, "row", axis=1, tiled=True),
        preferred_element_type=jnp.float32,
    )
    return running / math.sqrt(rows_total)


def solution(mesh):
    return jax.shard_map(
        local,
        mesh=mesh,
        in_specs=(
            P(("grp", "freq"), "row", "col"),
            P(("grp", "row"), None),
            P(("grp", "col", "freq"), None),
            P("grp", None),
        ),
        out_specs=P("grp", "row", ("col", "freq")),
        check_vma=False,
    )
```

profile of v0, /device:TPU:0, one launch (start us, length us, event | category | flops | bytes accessed | tf_op | source)
XLA Modules:
  0.0 149.0 jit_solution(16432241815298372039)
XLA Ops:
  6.5 11.6 %copy.15 = bf16[16,72,2048]{1,0,2:T(8,128)(2,1)} copy(bf16[16,72,2048]{2,1,0:T(8,128)(2,1)} %param.4) | data formatting | bytes 9437184 | tf_op args[0]
  18.1 6.9 %all-to-all-start = ((bf16[16,72,2048]{1,0,2:T(8,128)(2,1)}), bf16[16,72,2048]{1,0,2:T(8,128)(2,1)}, u32[]{:S(2)}, u32[]{:S(2)}) async-start(bf16[16,72,2048]{1,0,2:T(8,128)(2,1)} %copy.15), calls=%async_computation | async-start | bytes 16777216 | tf_op jit(solution)/shard_map/all_to_all | solution.py:24
  25.1 0.0 reduce-scatter.2.cloned.1.call-start
  25.2 7.4 %all-to-all-done = bf16[16,72,2048]{1,0,2:T(8,128)(2,1)} async-done(((bf16[16,72,2048]{1,0,2:T(8,128)(2,1)}), bf16[16,72,2048]{1,0,2:T(8,128)(2,1)}, u32[]{:S(2)}, u32[]{:S(2)}) %all-to-all-start) | async-done | bytes 4718624 | tf_op jit(solution)/shard_map/all_to_all | solution.py:24
  32.6 0.0 copy-start
  32.6 11.6 %copy.16 = bf16[16,72,2,1024]{3,1,0,2:T(8,128)(2,1)} copy(bf16[16,72,2,1024]{1,0,3,2:T(8,128)(2,1)} %bitcast.2) | data formatting | bytes 9437184 | tf_op jit(solution)/shard_map/all_to_all | solution.py:24
  44.2 0.0 copy-done
  44.2 0.0 copy-start.1
  44.2 8.9 %fusion = f32[4,72,1024]{2,0,1:T(4,128)S(1)} fusion(f32[4]{0:T(128)S(1)} %add_multiply_fusion, f32[32]{0:T(128)S(1)} %compare_select_fusion, bf16[4,8,72,1024]{3,2,1,0:T(8,128)(2,1)} %bitcast.45), kind=kOutput, calls=%fused_computation | convolution fusion | flops 113246720 | bytes 5898384 | tf_op jit(solution)/shard_map/dot_general | solution.py:26
  53.1 0.0 copy-done.1
  53.1 8.2 %fusion.7 = f32[4,72,2048]{2,1,0:T(8,128)} fusion(bf16[1024,2048]{1,0:T(8,128)(2,1)} %param.6, f32[4,72,1024]{2,0,1:T(4,128)S(1)} %fusion, f32[4,2048]{1,0:T(4,128)S(1)} %copy-done.1, f32[72,2048]{1,0:T(8,128)S(1)} %convert_element_type.13), kind=kOutput, calls=%fused_computation.8 | convolution fusion | flops 2418573312 | bytes 8355840 | tf_op jit(solution)/shard_map/tpq,qj->tpj/dot_general | solution.py:34
  61.3 0.0 reduce-scatter.2.cloned.1.call-update
  61.3 0.0 all-gather.2.cloned.1.call-start
  61.4 35.8 %reduce-scatter.2.cloned.1.call-done = f32[4,72,512]{2,1,0:T(8,128)} async-done(((f32[4,72,2048]{2,1,0:T(8,128)}), f32[4,72,512]{2,1,0:T(8,128)}) %reduce-scatter.2.cloned.1.call-update) | async-done | bytes 589840 | tf_op jit(solution)/shard_map/reduce_scatter | solution.py:37
  97.2 1.8 %convert_element_type.16 = bf16[4,72,512]{2,1,0:T(8,128)(2,1)} convert(f32[4,72,512]{2,1,0:T(8,128)} %reduce-scatter.2.cloned.1.call-done) | non-fusion elementwise | flops 147456 | bytes 884736 | tf_op jit(solution)/shard_map/convert_element_type | solution.py:39
  99.0 0.0 all-gather.2.cloned.1.call-update
  99.1 19.4 %all_to_all.34 = bf16[72,4,512]{2,0,1:T(8,128)(2,1)S(1)} all-to-all(bf16[72,4,512]{2,0,1:T(8,128)(2,1)S(1)} %bitcast.48), channel_id=1, replica_groups=mesh['grp'=2,'row'=4,'col'=2,'freq'=2] {'row'}, dimensions={1} | all-to-all | bytes 589824 | tf_op jit(solution)/shard_map/all_to_all | solution.py:40
  118.4 14.0 %all-gather.2.cloned.1.call-done = bf16[4,288,512]{2,1,0:T(8,128)(2,1)} async-done(((bf16[4,72,512]{2,1,0:T(8,128)(2,1)}), bf16[4,288,512]{2,1,0:T(8,128)(2,1)}) %all-gather.2.cloned.1.call-update) | async-done | bytes 1179664 | tf_op jit(solution)/shard_map/all_gather | solution.py:45
  132.4 4.5 %multiply_bitcast_fusion = f32[4,512,512]{1,2,0:T(8,128)} fusion(bf16[4,288,512]{2,1,0:T(8,128)(2,1)} %all-gather.2.cloned.1.call-done, bf16[288,512,1]{1,0,2:T(8,128)(2,1)S(1)} %bitcast.46), kind=kOutput, calls=%fused_computation.7 | convolution fusion | flops 605028352 | bytes 5668864 | tf_op jit(solution)/shard_map/pi,tpj->tij/dot_general | solution.py:42
  136.9 5.2 %copy.20 = f32[4,512,512]{2,1,0:T(8,128)} copy(f32[4,512,512]{1,2,0:T(8,128)} %multiply_bitcast_fusion) | data formatting | bytes 8388608 | tf_op jit(solution)/shard_map/div | solution.py:48
  (4 shorter events, 0.1 us)
Async XLA Ops:
  18.1 14.4 %all-to-all-start = ((bf16[16,72,2048]{1,0,2:T(8,128)(2,1)}), bf16[16,72,2048]{1,0,2:T(8,128)(2,1)}, u32[]{:S(2)}, u32[]{:S(2)}) async-start(bf16[16,72,2048]{1,0,2:T(8,128)(2,1)} %copy.15), calls=%async_computation | async-start | bytes 16777216 | tf_op jit(solution)/shard_map/all_to_all | solution.py:24
  25.1 72.1 %reduce-scatter.2.cloned.1.call-start = ((), (), s32[]{:S(2)}) async-start(), calls=%async_computation.3 | async-start | bytes 2949120 | tf_op jit(solution)/shard_map/reduce_scatter | solution.py:37
  32.6 11.6 %copy-start = (bf16[72,2048]{1,0:T(8,128)(2,1)S(1)}, bf16[72,2048]{1,0:T(8,128)(2,1)}, u32[]{:S(2)}) copy-start(bf16[72,2048]{1,0:T(8,128)(2,1)} %param.5) | copy-start | bytes 884740
  44.2 8.9 %copy-start.1 = (f32[4,2048]{1,0:T(4,128)S(1)}, f32[4,2048]{1,0:T(4,128)}, u32[]{:S(2)}) copy-start(f32[4,2048]{1,0:T(4,128)} %param.7) | copy-start | bytes 98308
  61.3 71.1 %all-gather.2.cloned.1.call-start = ((), (), s32[]{:S(2)}) async-start(), calls=%async_computation.4 | async-start | bytes 1474560 | tf_op jit(solution)/shard_map/all_gather | solution.py:45
Sparse Core Ops, SparseCore 0:
  61.4 35.7 reduce-scatter.1
  99.2 33.1 all-gather.1
where the time goes:
time: 150 us; the launch traced here: 149 us
  waiting for transfers between devices  57.2 us (38%)
  local copies, waits for them, and re-layouts  28.5 us (19%)
  matrix products  21.6 us (14%)
  blocking collectives  19.4 us (13%)
  between operations  13.5 us (9%)
  starting transfers between devices  7.02 us (5%)
  other arithmetic  1.87 us (1%)
    reduce_scatter x1, waiting for transfers between devices, local(): lax.psum_scatter(half_terms, ('col', 'freq'), scatter_dimension=2, tiled=...  35.8 us
    all_to_all x1, blocking collectives, local(): lax.all_to_all(x_rows, 'row', split_axis=1, concat_axis=0, tiled=True)  19.4 us
    all_gather x1, waiting for transfers between devices, local(): lax.all_gather(half_proj, 'row', axis=1, tiled=True)  14 us
    all_to_all x1, local copies, waits for them, and re-layouts, local(): lax.all_to_all(w_freq, 'freq', split_axis=2, concat_axis=0, tiled=True)  11.6 us
    unnamed x5, local copies, waits for them, and re-layouts  11.6 us
    dot_general x1, matrix products, local(): jnp.dot(transform, flattened, precision=lax.Precision.HIGHEST)  8.88 us
    dot_general x1, matrix products, local(): jnp.einsum('tpq,qj->tpj', sigma_tau, x_cols, preferred_element_type=jnp.f...  8.18 us
    all_to_all x1, waiting for transfers between devices, local(): lax.all_to_all(w_freq, 'freq', split_axis=2, concat_axis=0, tiled=True)  7.4 us
  transfers between devices with their start and end apart: 3, of which 3 were waited for; matrix products, arithmetic and copies ran while one was open for 0% of the time, Pallas kernels for 0%

commit v1 on v0

v1 whole, which is shorter than its diff:
```python
import functools
import math

import jax
import jax.numpy as jnp
from jax import lax
from jax.experimental import pallas as pl
from jax.experimental.pallas import tpu as pltpu
from jax.sharding import PartitionSpec as P

F32 = jnp.float32
BF16 = jnp.bfloat16
MESH = pl.DeviceIdType.MESH
CHUNK = 256
QBLOCK = 256


def remote(src, dst, send_sem, recv_sem, device):
    return pltpu.make_async_remote_copy(
        src_ref=src, dst_ref=dst, send_sem=send_sem, recv_sem=recv_sem,
        device_id=device, device_id_type=MESH,
    )


def coefficients(f, shards, per_shard, tau_count, extra):
    period = tau_count + 1
    norm = extra / math.sqrt(2.0 * shards * per_shard)

    def pick(values):
        out = jnp.float32(values[0])
        for s in range(1, shards):
            out = jnp.where(f == s, jnp.float32(values[s]), out)
        return out

    coef = [
        [
            pick([
                2.0 * norm * math.cos(2.0 * math.pi * (((a + 1) * (s * per_shard + m)) % period) / period)
                for s in range(shards)
            ])
            for m in range(period)
        ]
        for a in range(tau_count // 2)
    ]
    drop = pick([norm if s == 0 else 0.0 for s in range(shards)])
    return coef, drop


def gather_kernel(
    rows_axis, cols_axis, tau_count, x_rows, occ, w_hbm, xc_hbm, hp, rbt,
    wbuf, xc, wsend, wown, wrecv, scaled, sig, p_send, p_recv, keep, x_send, x_recv, rb,
    lsem, w_sem, p_ssem, p_rsem, x_ssem, x_rsem, b_ssem, b_rsem, z_ssem, z_rsem,
):
    R, C = rows_axis, cols_axis
    z, c, f = lax.axis_index("row"), lax.axis_index("col"), lax.axis_index("freq")
    pairs = tau_count // 2
    rows, norb = x_rows.shape
    per_shard = w_hbm.shape[0]
    Q = xc.shape[0]
    owned = norb // (2 * C)
    parts = owned // CHUNK
    n = pairs * parts
    win = rb.shape[2]
    ichunk = norb // R
    core = {"freq": 1 - f}

    loads = [
        pltpu.make_async_copy(w_hbm.at[:, :, pl.ds(pl.multiple_of((1 - f) * Q, 128), Q)], wbuf.at[0], lsem.at[0]),
        pltpu.make_async_copy(w_hbm.at[:, :, pl.ds(pl.multiple_of(f * Q, 128), Q)], wbuf.at[1], lsem.at[1]),
        pltpu.make_async_copy(xc_hbm, xc, lsem.at[2]),
    ]
    for load in loads:
        load.start()

    barrier = pltpu.get_barrier_semaphore()
    pl.semaphore_signal(barrier, inc=1, device_id=core, device_id_type=MESH)
    for s in range(1, C):
        pl.semaphore_signal(barrier, inc=1, device_id={"col": lax.rem(c + s, C)}, device_id_type=MESH)

    @pl.loop(1, R)
    def _(s):
        pl.semaphore_signal(barrier, inc=1, device_id={"row": lax.rem(z + s, R)}, device_id_type=MESH)

    pl.semaphore_wait(barrier, 1 + (C - 1) + (R - 1))

    def window(to):
        return pl.ds(pl.multiple_of((to * ichunk) // win * win, 128), win)

    def basis_copy(s):
        to = lax.rem(z + s, R)
        return remote(x_rows.at[:, window(to)], rb.at[z], b_ssem.at[s], b_rsem.at[s], {"row": to})

    def basis_arrival(s):
        return remote(
            x_rows.at[:, window(z)], rb.at[lax.rem(z - s + R, R)], b_ssem.at[s], b_rsem.at[s], {"row": lax.rem(z + s, R)}
        )

    @pl.loop(1, R)
    def _(s):
        basis_copy(s).start()

    own_basis = pltpu.make_async_copy(x_rows.at[:, window(z)], rb.at[z], lsem.at[3])
    own_basis.start()

    coef, drop = coefficients(f, 2, per_shard, tau_count, 1.0 / math.sqrt(norb))
    period = tau_count + 1

    def fold(src, dst):
        @pl.loop(0, Q // 128)
        def _(b):
            lanes = pl.ds(pl.multiple_of(b * 128, 128), 128)
            first = src[0, :, lanes].astype(F32)
            acc = [first * (-drop)] * pairs
            for m in range(period):
                total = first if m == 0 else src[m, :, lanes].astype(F32)
                for i in range(m + period, per_shard, period):
                    total = total + src[i, :, lanes].astype(F32)
                acc = [acc[a] + total * coef[a][m] for a in range(pairs)]
            for a in range(pairs):
                dst[a, :, lanes] = acc[a]

    loads[0].wait()
    fold(wbuf.at[0], wsend)
    w_copy = remote(wsend, wrecv, w_sem.at[0], w_sem.at[1], core)
    w_copy.start()
    loads[1].wait()
    fold(wbuf.at[1], wown)
    for a in range(pairs):
        xr = x_rows[...].astype(F32)
        scaled[a] = jnp.concatenate(
            [xr * occ[a : a + 1, :], xr * occ[tau_count - 1 - a : tau_count - a, :]], axis=0
        ).astype(BF16)
    loads[2].wait()
    w_copy.wait_recv()

    def green(a):
        @pl.loop(0, Q // QBLOCK)
        def _(b):
            block = pl.ds(pl.multiple_of(b * QBLOCK, QBLOCK), QBLOCK)
            g = lax.dot_general(
                scaled[a], xc[block, :], (((1,), (1,)), ((), ())), preferred_element_type=F32
            )
            w = wown[a, :, block] + wrecv[a, :, block]
            sig[a, :, block] = (g * jnp.concatenate([w, w], axis=0)).astype(BF16)

    def p_copy(k):
        return remote(p_send.at[k], p_recv.at[k], p_ssem.at[k], p_rsem.at[k], core)

    def x_copy(k, s):
        return remote(
            x_send.at[k, s - 1], x_recv.at[k, s - 1], x_ssem.at[k, s - 1], x_rsem.at[k, s - 1],
            {"col": lax.rem(c + s, C)},
        )

    def partial(k):
        a, m = divmod(k, parts)

        def dot(s, ff):
            off = pl.multiple_of((lax.rem(c + s, C) * 2 + ff) * owned + m * CHUNK, CHUNK)
            return jnp.dot(sig[a], xc[:, pl.ds(off, CHUNK)], preferred_element_type=F32)

        for s in range(C):
            p_send[k, s] = dot(s, 1 - f).astype(BF16)
        p_copy(k).start()
        for s in range(C):
            keep[k, s] = dot(s, f)

    def across(k):
        p_copy(k).wait_recv()
        for s in range(1, C):
            x_send[k, s - 1] = (keep[k, s] + p_recv[k, s].astype(F32)).astype(BF16)
            x_copy(k, s).start()

    def to_right(d, k):
        o = jnp.maximum(z - d, 0)
        return remote(hp.at[o, k], hp.at[o, k], z_ssem.at[0, d, k], z_rsem.at[0, d, k], {"row": jnp.minimum(z + 1, R - 1)})

    def to_left(d, k):
        o = jnp.minimum(z + d, R - 1)
        return remote(hp.at[o, k], hp.at[o, k], z_ssem.at[1, d, k], z_rsem.at[1, d, k], {"row": jnp.maximum(z - 1, 0)})

    def from_left(d, k):
        o = jnp.maximum(z - d, 0)
        return remote(hp.at[o, k], hp.at[o, k], z_ssem.at[0, d - 1, k], z_rsem.at[0, d - 1, k], {"row": jnp.minimum(z + 1, R - 1)})

    def from_right(d, k):
        o = jnp.minimum(z + d, R - 1)
        return remote(hp.at[o, k], hp.at[o, k], z_ssem.at[1, d - 1, k], z_rsem.at[1, d - 1, k], {"row": jnp.maximum(z - 1, 0)})

    scale = 1.0 / math.sqrt(2.0 * C * Q)

    def finish(k):
        total = keep[k, 0] + p_recv[k, 0].astype(F32)
        for s in range(1, C):
            x_copy(k, s).wait_recv()
            total = total + x_recv[k, s - 1].astype(F32)
        hp[z, k] = (total * scale).astype(BF16)

        @pl.when(z < R - 1)
        def _():
            to_right(0, k).start()

        @pl.when(z > 0)
        def _():
            to_left(0, k).start()

    for k in range(n + 2):
        if k < n:
            if k % parts == 0:
                green(k // parts)
            partial(k)
        if 1 <= k <= n:
            across(k - 1)
        if k >= 2:
            finish(k - 2)

    own_basis.wait()

    @pl.loop(1, R)
    def _(s):
        basis_arrival(s).wait_recv()

    rbt[...] = jnp.concatenate([rb[s].astype(F32) for s in range(R)], axis=0).T.astype(BF16)

    @pl.loop(1, R)
    def _(d):
        for k in range(n):
            @pl.when(z - d >= 0)
            def _():
                from_left(d, k).wait_recv()

                @pl.when(z < R - 1)
                def _():
                    to_right(d, k).start()

            @pl.when(z + d <= R - 1)
            def _():
                from_right(d, k).wait_recv()

                @pl.when(z > 0)
                def _():
                    to_left(d, k).start()

    w_copy.wait_send()
    for k in range(n):
        p_copy(k).wait_send()
        for s in range(1, C):
            x_copy(k, s).wait_send()

    @pl.loop(1, R)
    def _(s):
        basis_copy(s).wait_send()

    @pl.loop(0, R)
    def _(d):
        for k in range(n):
            @pl.when((z - d >= 0) & (z < R - 1))
            def _():
                to_right(d, k).wait_send()

            @pl.when((z + d <= R - 1) & (z > 0))
            def _():
                to_left(d, k).wait_send()


def project_kernel(rows_axis, tau_count, ichunk, hp, rbt, out):
    R = rows_axis
    t = pl.program_id(0)
    z = lax.axis_index("row")
    parts = hp.shape[1] // (tau_count // 2)
    rows = hp.shape[2] // 2
    a = jnp.minimum(t, tau_count - 1 - t)
    upper = t >= tau_count // 2
    blocks = []
    for s in range(R):
        both = jnp.concatenate([hp[s, a * parts + m].astype(F32) for m in range(parts)], axis=1)
        blocks.append(jnp.where(upper, both[rows:], both[:rows]))
    right = jnp.concatenate(blocks, axis=0).astype(BF16)
    start = pl.multiple_of(lax.rem(z * ichunk, rbt.shape[0]), min(ichunk, rbt.shape[0]))
    left = rbt[...] if ichunk == rbt.shape[0] else rbt[pl.ds(start, ichunk), :]
    out[0] = jnp.dot(left, right, preferred_element_type=F32) * (1.0 / math.sqrt(R * rows))


def local(rows_axis, cols_axis, w_freq, x_rows, x_cols, occupation):
    R, C = rows_axis, cols_axis
    per_shard, rows, wide = w_freq.shape
    tau_count, norb = occupation.shape
    Q = x_cols.shape[0]
    pairs = tau_count // 2
    owned = norb // (2 * C)
    n = pairs * (owned // CHUNK)
    ichunk = norb // R
    win = max(ichunk, 128)
    dma = pltpu.SemaphoreType.DMA
    vmem = pl.BlockSpec(memory_space=pltpu.VMEM)
    anywhere = pl.BlockSpec(memory_space=pl.ANY)
    hp, rbt = pl.pallas_call(
        functools.partial(gather_kernel, R, C, tau_count),
        out_shape=(
            jax.ShapeDtypeStruct((R, n, 2 * rows, CHUNK), BF16),
            jax.ShapeDtypeStruct((win, R * rows), BF16),
        ),
        in_specs=[vmem, vmem, anywhere, anywhere],
        out_specs=(vmem, vmem),
        scratch_shapes=[
            pltpu.VMEM((2, per_shard, rows, Q), BF16),
            pltpu.VMEM((Q, norb), BF16),
            pltpu.VMEM((pairs, rows, Q), F32),
            pltpu.VMEM((pairs, rows, Q), F32),
            pltpu.VMEM((pairs, rows, Q), F32),
            pltpu.VMEM((pairs, 2 * rows, norb), BF16),
            pltpu.VMEM((pairs, 2 * rows, Q), BF16),
            pltpu.VMEM((n, C, 2 * rows, CHUNK), BF16),
            pltpu.VMEM((n, C, 2 * rows, CHUNK), BF16),
            pltpu.VMEM((n, C, 2 * rows, CHUNK), F32),
            pltpu.VMEM((n, C - 1, 2 * rows, CHUNK), BF16),
            pltpu.VMEM((n, C - 1, 2 * rows, CHUNK), BF16),
            pltpu.VMEM((R, rows, win), BF16),
            dma((4,)),
            dma((2,)),
            dma((n,)),
            dma((n,)),
            dma((n, C - 1)),
            dma((n, C - 1)),
            dma((R,)),
            dma((R,)),
            dma((2, R, n)),
            dma((2, R, n)),
        ],
        compiler_params=pltpu.CompilerParams(
            collective_id=0, has_side_effects=True, vmem_limit_bytes=44 * 1024 * 1024
        ),
        name="gather_half",
    )(x_rows, occupation, w_freq, x_cols)
    return pl.pallas_call(
        functools.partial(project_kernel, R, tau_count, ichunk),
        grid=(tau_count,),
        out_shape=jax.ShapeDtypeStruct((tau_count, ichunk, owned), F32),
        in_specs=[
            pl.BlockSpec(hp.shape, lambda t: (0, 0, 0, 0)),
            pl.BlockSpec(rbt.shape, lambda t: (0, 0)),
        ],
        out_specs=pl.BlockSpec((1, ichunk, owned), lambda t: (t, 0, 0)),
        compiler_params=pltpu.CompilerParams(vmem_limit_bytes=48 * 1024 * 1024),
        name="project",
    )(hp, rbt)


def solution(mesh):
    assert mesh.shape["freq"] == 2
    return jax.shard_map(
        functools.partial(local, mesh.shape["row"], mesh.shape["col"]),
        mesh=mesh,
        in_specs=(
            P(("grp", "freq"), "row", "col"),
            P(("grp", "row"), None),
            P(("grp", "col", "freq"), None),
            P("grp", None),
        ),
        out_specs=P("grp", "row", ("col", "freq")),
        check_vma=False,
    )
```

time: 150 us -> 45.6 us (0.30)
  waiting for transfers between devices: 57.2 us -> 0 us
  Pallas kernels: 0 us -> 41.4 us
  local copies, waits for them, and re-layouts: 28.5 us -> 3.91 us
  matrix products: 21.6 us -> 0 us
  blocking collectives: 19.4 us -> 0 us
  between operations: 13.5 us -> 0.01 us
  starting transfers between devices: 7.02 us -> 0 us
  other arithmetic: 1.87 us -> 0 us
    pallas_call x0 -> x2, Pallas kernels: none -> 41.4 us  [the longest x1 38 us: local(): pl.pallas_call(functools.partial(gather_kernel, R, C, tau_count), out_sha...]
    reduce_scatter x1 -> x0, waiting for transfers between devices: 35.8 us -> none  [local(): lax.psum_scatter(half_terms, ('col', 'freq'), scatter_dimension=2, tiled=...]
    dot_general x3 -> x0, matrix products: 21.6 us -> none  [the longest x1 8.88 us: local(): jnp.dot(transform, flattened, precision=lax.Precision.HIGHEST)]
    all_to_all x1 -> x0, blocking collectives: 19.4 us -> none  [local(): lax.all_to_all(x_rows, 'row', split_axis=1, concat_axis=0, tiled=True)]
    all_gather x1 -> x0, waiting for transfers between devices: 14 us -> none  [local(): lax.all_gather(half_proj, 'row', axis=1, tiled=True)]
    all_to_all x2 -> x0, local copies, waits for them, and re-layouts: 11.6 us -> none  [the longest x1 11.6 us: local(): lax.all_to_all(w_freq, 'freq', split_axis=2, concat_axis=0, tiled=True)]
    unnamed x5 -> x6, local copies, waits for them, and re-layouts: 11.6 us -> 3.91 us
    all_to_all x1 -> x0, waiting for transfers between devices: 7.4 us -> none  [local(): lax.all_to_all(w_freq, 'freq', split_axis=2, concat_axis=0, tiled=True)]
  transfers between devices with their start and end apart: 3 -> 0, of which waited for: 3 -> 0; matrix products, arithmetic and copies ran while one was open for 0% -> 0% of each run, Pallas kernels for 0% -> 0%
where the time goes in v1:
time: 45.6 us; the launch traced here: 45.3 us
  Pallas kernels  41.4 us (91%)
  local copies, waits for them, and re-layouts  3.91 us (9%)
    pallas_call x1, Pallas kernels, local(): pl.pallas_call(functools.partial(gather_kernel, R, C, tau_count), out_sha...  38 us
    unnamed x6, local copies, waits for them, and re-layouts  3.91 us
    pallas_call x1, Pallas kernels, local(): pl.pallas_call(functools.partial(project_kernel, R, tau_count, ichunk), g...  3.37 us

profile of v1, /device:TPU:0, one launch (start us, length us, event | category | flops | bytes accessed | tf_op | source)
XLA Modules:
  0.0 45.3 jit_solution(4831197121446199156)
XLA Ops:
  0.0 0.0 copy-start
  0.0 2.2 %copy-done = bf16[1024,2048]{1,0:T(8,128)(2,1)S(1)} copy-done((bf16[1024,2048]{1,0:T(8,128)(2,1)S(1)}, bf16[1024,2048]{1,0:T(8,128)(2,1)}, u32[]{:S(2)}) %copy-start) | copy-done | bytes 4194328
  2.2 0.0 copy-start.1
  2.2 1.0 %copy-done.1 = bf16[72,2048]{1,0:T(8,128)(2,1)S(1)} copy-done((bf16[72,2048]{1,0:T(8,128)(2,1)S(1)}, bf16[72,2048]{1,0:T(8,128)(2,1)}, u32[]{:S(2)}) %copy-start.1) | copy-done | bytes 294936
  3.2 0.0 copy-start.2
  3.2 0.8 %copy-done.2 = f32[4,2048]{1,0:T(4,128)S(1)} copy-done((f32[4,2048]{1,0:T(4,128)S(1)}, f32[4,2048]{1,0:T(4,128)}, u32[]{:S(2)}) %copy-start.2) | copy-done | bytes 32792
  3.9 38.0 %gather_half.1 = (bf16[4,4,144,256]{3,2,1,0:T(8,128)(2,1)S(1)}, bf16[512,288]{1,0:T(8,128)(2,1)S(1)}) custom-call(bf16[72,2048]{1,0:T(8,128)(2,1)S(1)} %copy-done.1, f32[4,2048]{1,0:T(4,128)S(1)} %copy-done.2, bf16[16,72,2048]{2,1,0:T(8,128)(2,1)} %w_hbm.1, bf16[1024,2048]{1,0:T(8,128)(2,1)S(1)} %copy-done), custom_call_target="tpu_custom_call" | custom-call | tf_op jit(solution)/shard_map/gather_half/pallas_call | solution.py:297
  41.9 3.4 %project.1 = f32[4,512,512]{2,1,0:T(8,128)} custom-call(bf16[4,4,144,256]{3,2,1,0:T(8,128)(2,1)S(1)} %get-tuple-element.7.hp, bf16[512,288]{1,0:T(8,128)(2,1)S(1)} %get-tuple-element.8.rbt), custom_call_target="tpu_custom_call" | custom-call | tf_op jit(solution)/shard_map/project/pallas_call | solution.py:335
Async XLA Ops:
  0.0 2.2 %copy-start = (bf16[1024,2048]{1,0:T(8,128)(2,1)S(1)}, bf16[1024,2048]{1,0:T(8,128)(2,1)}, u32[]{:S(2)}) copy-start(bf16[1024,2048]{1,0:T(8,128)(2,1)} %xc_hbm.1) | copy-start | bytes 12582916
  2.2 1.0 %copy-start.1 = (bf16[72,2048]{1,0:T(8,128)(2,1)S(1)}, bf16[72,2048]{1,0:T(8,128)(2,1)}, u32[]{:S(2)}) copy-start(bf16[72,2048]{1,0:T(8,128)(2,1)} %x_rows.1) | copy-start | bytes 884740
  3.2 0.8 %copy-start.2 = (f32[4,2048]{1,0:T(4,128)S(1)}, f32[4,2048]{1,0:T(4,128)}, u32[]{:S(2)}) copy-start(f32[4,2048]{1,0:T(4,128)} %occ.1) | copy-start | bytes 98308

commit v2 on v1

v2 whole, which is shorter than its diff:
```python
import functools
import math

import jax
import jax.numpy as jnp
from jax import lax
from jax.experimental import pallas as pl
from jax.experimental.pallas import tpu as pltpu
from jax.sharding import PartitionSpec as P

F32 = jnp.float32
BF16 = jnp.bfloat16
MESH = pl.DeviceIdType.MESH
CHUNK = 256
QBLOCK = 256
WPARTS = 2
GATHER_VMEM = 52 * 1024 * 1024
PROJECT_VMEM = 40 * 1024 * 1024


def remote(src, dst, send_sem, recv_sem, device):
    return pltpu.make_async_remote_copy(
        src_ref=src, dst_ref=dst, send_sem=send_sem, recv_sem=recv_sem,
        device_id=device, device_id_type=MESH,
    )


def coefficients(f, shards, per_shard, tau_count, extra):
    period = tau_count + 1
    norm = extra / math.sqrt(2.0 * shards * per_shard)

    def pick(values):
        out = jnp.float32(values[0])
        for s in range(1, shards):
            out = jnp.where(f == s, jnp.float32(values[s]), out)
        return out

    coef = [
        [
            pick([
                2.0 * norm * math.cos(2.0 * math.pi * (((a + 1) * (s * per_shard + m)) % period) / period)
                for s in range(shards)
            ])
            for m in range(period)
        ]
        for a in range(tau_count // 2)
    ]
    drop = pick([norm if s == 0 else 0.0 for s in range(shards)])
    return coef, drop


def gather_kernel(
    rows_axis, cols_axis, tau_count, xr_hbm, occ_hbm, w_hbm, xc_hbm, hp, rbt,
    x_rows, occ, wbuf, xc, wsend, wown, wrecv, scaled, gbuf, sig, p_send, p_recv, keep, x_send, x_recv, rb,
    lsem, w_ssem, w_rsem, p_ssem, p_rsem, x_ssem, x_rsem, b_ssem, b_rsem, z_ssem, z_rsem,
):
    R, C = rows_axis, cols_axis
    z, c, f = lax.axis_index("row"), lax.axis_index("col"), lax.axis_index("freq")
    pairs = tau_count // 2
    rows, norb = x_rows.shape
    per_shard = w_hbm.shape[0]
    Q = xc.shape[0]
    owned = norb // (2 * C)
    parts = owned // CHUNK
    n = pairs * parts
    shares = rb.shape[0]
    win = rb.shape[3] * shares
    half = Q // WPARTS
    ichunk = norb // R
    core = {"freq": 1 - f}

    def w_load(h, q):
        owner = 1 - f if h == 0 else f
        lanes = pl.ds(pl.multiple_of(owner * Q + q * half, 128), half)
        return pltpu.make_async_copy(w_hbm.at[:, :, lanes], wbuf.at[h, q], lsem.at[h * WPARTS + q])

    rows_load = pltpu.make_async_copy(xr_hbm, x_rows, lsem.at[2 * WPARTS])
    occ_load = pltpu.make_async_copy(occ_hbm, occ, lsem.at[2 * WPARTS + 1])
    xc_load = pltpu.make_async_copy(xc_hbm, xc, lsem.at[2 * WPARTS + 2])
    rows_load.start()
    occ_load.start()
    for q in range(WPARTS):
        w_load(0, q).start()
    for q in range(WPARTS):
        w_load(1, q).start()
    xc_load.start()

    barrier = pltpu.get_barrier_semaphore()
    pl.semaphore_signal(barrier, inc=1, device_id=core, device_id_type=MESH)
    for s in range(1, C):
        pl.semaphore_signal(barrier, inc=1, device_id={"col": lax.rem(c + s, C)}, device_id_type=MESH)

    @pl.loop(1, R)
    def _(s):
        pl.semaphore_signal(barrier, inc=1, device_id={"row": lax.rem(z + s, R)}, device_id_type=MESH)

    pl.semaphore_wait(barrier, 1 + (C - 1) + (R - 1))

    rows_load.wait()
    piece = win // shares
    mine = f if shares == 2 else 0

    def window(to):
        start = (to * ichunk) // win * win + mine * piece
        return pl.ds(pl.multiple_of(start, 128), piece)

    def basis_copy(s):
        to = lax.rem(z + s, R)
        return remote(x_rows.at[:, window(to)], rb.at[mine, z], b_ssem.at[s], b_rsem.at[s], {"row": to})

    def basis_arrival(s):
        return remote(
            x_rows.at[:, window(z)], rb.at[mine, lax.rem(z - s + R, R)], b_ssem.at[s], b_rsem.at[s],
            {"row": lax.rem(z + s, R)},
        )

    @pl.loop(1, R)
    def _(s):
        basis_copy(s).start()

    own_basis = pltpu.make_async_copy(x_rows.at[:, window(z)], rb.at[mine, z], lsem.at[2 * WPARTS + 3])
    own_basis.start()

    def basis_share(which):
        return remote(rb.at[which], rb.at[which], b_ssem.at[0], b_rsem.at[0], core)

    def basis_gathered():
        own_basis.wait()

        @pl.loop(1, R)
        def _(s):
            basis_arrival(s).wait_recv()

        if shares == 2:
            basis_share(mine).start()

    def basis_done():
        if shares == 2:
            basis_share(1 - mine).wait_recv()
        sides = [
            jnp.concatenate([rb[h, s].astype(F32) for s in range(R)], axis=0) for h in range(shares)
        ]
        for h in range(shares):
            rbt[h * piece : (h + 1) * piece, :] = sides[h].T.astype(BF16)

    coef, drop = coefficients(f, 2, per_shard, tau_count, 1.0 / math.sqrt(norb))
    period = tau_count + 1

    def fold(src, dst):
        @pl.loop(0, half // 128)
        def _(b):
            lanes = pl.ds(pl.multiple_of(b * 128, 128), 128)
            first = src[0, :, lanes].astype(F32)
            acc = [first * (-drop)] * pairs
            for m in range(period):
                total = first if m == 0 else src[m, :, lanes].astype(F32)
                for i in range(m + period, per_shard, period):
                    total = total + src[i, :, lanes].astype(F32)
                acc = [acc[a] + total * coef[a][m] for a in range(pairs)]
            for a in range(pairs):
                dst[a, :, lanes] = acc[a]

    def w_copy(q):
        return remote(wsend.at[q], wrecv.at[q], w_ssem.at[q], w_rsem.at[q], core)

    for q in range(WPARTS):
        w_load(0, q).wait()
        fold(wbuf.at[0, q], wsend.at[q])
        w_copy(q).start()
    occ_load.wait()

    def scale_rows(a):
        xr = x_rows[...].astype(F32)
        scaled[a] = jnp.concatenate(
            [xr * occ[a : a + 1, :], xr * occ[tau_count - 1 - a : tau_count - a, :]], axis=0
        ).astype(BF16)

    scale_rows(0)
    for q in range(WPARTS):
        w_load(1, q).wait()
        fold(wbuf.at[1, q], wown.at[q])
    for a in range(1, pairs):
        scale_rows(a)
    xc_load.wait()

    def green(a):
        for b in range(Q // QBLOCK):
            block = pl.ds(b * QBLOCK, QBLOCK)
            gbuf[:, block] = lax.dot_general(
                scaled[a], xc[block, :], (((1,), (1,)), ((), ())), preferred_element_type=F32
            )

    def weigh(a):
        for q in range(WPARTS):
            if a == 0:
                w_copy(q).wait_recv()
            w = wown[q, a] + wrecv[q, a]
            block = pl.ds(q * half, half)
            sig[a, :, block] = (gbuf[:, block] * jnp.concatenate([w, w], axis=0)).astype(BF16)

    def p_copy(k, s):
        return remote(p_send.at[k, s], p_recv.at[k, s], p_ssem.at[k, s], p_rsem.at[k, s], core)

    def x_copy(k, s):
        return remote(
            x_send.at[k, s - 1], x_recv.at[k, s - 1], x_ssem.at[k, s - 1], x_rsem.at[k, s - 1],
            {"col": lax.rem(c + s, C)},
        )

    order = list(range(1, C)) + [0]

    def partial(k):
        a, m = divmod(k, parts)

        def dot(s, ff):
            off = pl.multiple_of((lax.rem(c + s, C) * 2 + ff) * owned + m * CHUNK, CHUNK)
            return jnp.dot(sig[a], xc[:, pl.ds(off, CHUNK)], preferred_element_type=F32)

        for s in order:
            p_send[k, s] = dot(s, 1 - f).astype(BF16)
            p_copy(k, s).start()
        for s in order:
            keep[k, s] = dot(s, f)

    def across(k):
        for s in range(1, C):
            p_copy(k, s).wait_recv()
            x_send[k, s - 1] = (keep[k, s] + p_recv[k, s].astype(F32)).astype(BF16)
            x_copy(k, s).start()

    def to_right(d, k):
        o = jnp.maximum(z - d, 0)
        return remote(hp.at[o, k], hp.at[o, k], z_ssem.at[0, d, k], z_rsem.at[0, d, k], {"row": jnp.minimum(z + 1, R - 1)})

    def to_left(d, k):
        o = jnp.minimum(z + d, R - 1)
        return remote(hp.at[o, k], hp.at[o, k], z_ssem.at[1, d, k], z_rsem.at[1, d, k], {"row": jnp.maximum(z - 1, 0)})

    def from_left(d, k):
        o = jnp.maximum(z - d, 0)
        return remote(hp.at[o, k], hp.at[o, k], z_ssem.at[0, d - 1, k], z_rsem.at[0, d - 1, k], {"row": jnp.minimum(z + 1, R - 1)})

    def from_right(d, k):
        o = jnp.minimum(z + d, R - 1)
        return remote(hp.at[o, k], hp.at[o, k], z_ssem.at[1, d - 1, k], z_rsem.at[1, d - 1, k], {"row": jnp.maximum(z - 1, 0)})

    scale = 1.0 / math.sqrt(2.0 * C * Q)

    def finish(k):
        p_copy(k, 0).wait_recv()
        total = keep[k, 0] + p_recv[k, 0].astype(F32)
        for s in range(1, C):
            x_copy(k, s).wait_recv()
            total = total + x_recv[k, s - 1].astype(F32)
        hp[z, k] = (total * scale).astype(BF16)

        @pl.when(z < R - 1)
        def _():
            to_right(0, k).start()

        @pl.when(z > 0)
        def _():
            to_left(0, k).start()

    def forward(d, k):
        @pl.when(z - d >= 0)
        def _():
            from_left(d, k).wait_recv()

            @pl.when(z < R - 1)
            def _():
                to_right(d, k).start()

        @pl.when(z + d <= R - 1)
        def _():
            from_right(d, k).wait_recv()

            @pl.when(z > 0)
            def _():
                to_left(d, k).start()

    for k in range(n + 2):
        if k < n:
            if k == 0:
                green(0)
                weigh(0)
            partial(k)
        if 1 <= k <= n:
            across(k - 1)
        if k % parts == parts - 1 and k + 1 < n:
            green((k + 1) // parts)
            weigh((k + 1) // parts)
        if k >= 2:
            finish(k - 2)
        if k == 2:
            basis_gathered()
    if n < 2:
        basis_gathered()
    basis_done()

    @pl.loop(1, R)
    def _(d):
        for k in range(n):
            forward(d, k)

    for q in range(WPARTS):
        w_copy(q).wait_send()
    if shares == 2:
        basis_share(mine).wait_send()
    for k in range(n):
        for s in range(C):
            p_copy(k, s).wait_send()
        for s in range(1, C):
            x_copy(k, s).wait_send()

    @pl.loop(1, R)
    def _(s):
        basis_copy(s).wait_send()

    @pl.loop(0, R)
    def _(d):
        for k in range(n):
            @pl.when((z - d >= 0) & (z < R - 1))
            def _():
                to_right(d, k).wait_send()

            @pl.when((z + d <= R - 1) & (z > 0))
            def _():
                to_left(d, k).wait_send()


def project_kernel(rows_axis, tau_count, ichunk, hp, rbt, out, obuf, sems):
    R = rows_axis
    z = lax.axis_index("row")
    pairs = tau_count // 2
    parts = hp.shape[1] // pairs
    rows = hp.shape[2] // 2
    start = pl.multiple_of(lax.rem(z * ichunk, rbt.shape[0]), min(ichunk, rbt.shape[0]))
    left = rbt[...] if ichunk == rbt.shape[0] else rbt[pl.ds(start, ichunk), :]
    scale = 1.0 / math.sqrt(R * rows)
    copies = []
    for a in range(pairs):
        both = [
            jnp.concatenate([hp[s, a * parts + m].astype(F32) for m in range(parts)], axis=1) for s in range(R)
        ]
        for t, first in ((a, 0), (tau_count - 1 - a, rows)):
            right = jnp.concatenate([b[first : first + rows] for b in both], axis=0).astype(BF16)
            for h in range(2):
                part = slice(h * ichunk // 2, (h + 1) * ichunk // 2)
                obuf[t, part, :] = jnp.dot(left[part], right, preferred_element_type=F32) * scale
                copies.append(pltpu.make_async_copy(obuf.at[t, part], out.at[t, part], sems.at[t, h]))
                copies[-1].start()
    for copy in copies:
        copy.wait()


def local(rows_axis, cols_axis, w_freq, x_rows, x_cols, occupation):
    R, C = rows_axis, cols_axis
    per_shard, rows, wide = w_freq.shape
    tau_count, norb = occupation.shape
    Q = x_cols.shape[0]
    pairs = tau_count // 2
    owned = norb // (2 * C)
    n = pairs * (owned // CHUNK)
    ichunk = norb // R
    win = max(ichunk, 128)
    shares = 2 if win % 256 == 0 else 1
    half = Q // WPARTS
    dma = pltpu.SemaphoreType.DMA
    vmem = pl.BlockSpec(memory_space=pltpu.VMEM)
    anywhere = pl.BlockSpec(memory_space=pl.ANY)
    hp, rbt = pl.pallas_call(
        functools.partial(gather_kernel, R, C, tau_count),
        out_shape=(
            jax.ShapeDtypeStruct((R, n, 2 * rows, CHUNK), BF16),
            jax.ShapeDtypeStruct((win, R * rows), BF16),
        ),
        in_specs=[anywhere] * 4,
        out_specs=(vmem, vmem),
        scratch_shapes=[
            pltpu.VMEM((rows, norb), BF16),
            pltpu.VMEM((tau_count, norb), F32),
            pltpu.VMEM((2, WPARTS, per_shard, rows, half), BF16),
            pltpu.VMEM((Q, norb), BF16),
            pltpu.VMEM((WPARTS, pairs, rows, half), F32),
            pltpu.VMEM((WPARTS, pairs, rows, half), F32),
            pltpu.VMEM((WPARTS, pairs, rows, half), F32),
            pltpu.VMEM((pairs, 2 * rows, norb), BF16),
            pltpu.VMEM((2 * rows, Q), F32),
            pltpu.VMEM((pairs, 2 * rows, Q), BF16),
            pltpu.VMEM((n, C, 2 * rows, CHUNK), BF16),
            pltpu.VMEM((n, C, 2 * rows, CHUNK), BF16),
            pltpu.VMEM((n, C, 2 * rows, CHUNK), F32),
            pltpu.VMEM((n, C - 1, 2 * rows, CHUNK), BF16),
            pltpu.VMEM((n, C - 1, 2 * rows, CHUNK), BF16),
            pltpu.VMEM((shares, R, rows, win // shares), BF16),
            dma((2 * WPARTS + 4,)),
            dma((WPARTS,)),
            dma((WPARTS,)),
            dma((n, C)),
            dma((n, C)),
            dma((n, C - 1)),
            dma((n, C - 1)),
            dma((R,)),
            dma((R,)),
            dma((2, R, n)),
            dma((2, R, n)),
        ],
        compiler_params=pltpu.CompilerParams(
            collective_id=0, has_side_effects=True, vmem_limit_bytes=GATHER_VMEM
        ),
        name="gather_half",
    )(x_rows, occupation, w_freq, x_cols)
    return pl.pallas_call(
        functools.partial(project_kernel, R, tau_count, ichunk),
        out_shape=jax.ShapeDtypeStruct((tau_count, ichunk, owned), F32),
        in_specs=[vmem, vmem],
        out_specs=anywhere,
        scratch_shapes=[pltpu.VMEM((tau_count, ichunk, owned), F32), dma((tau_count, 2))],
        compiler_params=pltpu.CompilerParams(vmem_limit_bytes=PROJECT_VMEM),
        name="project",
    )(hp, rbt)


def solution(mesh):
    assert mesh.shape["freq"] == 2
    return jax.shard_map(
        functools.partial(local, mesh.shape["row"], mesh.shape["col"]),
        mesh=mesh,
        in_specs=(
            P(("grp", "freq"), "row", "col"),
            P(("grp", "row"), None),
            P(("grp", "col", "freq"), None),
            P("grp", None),
        ),
        out_specs=P("grp", "row", ("col", "freq")),
        check_vma=False,
    )
```

time: 45.6 us -> 40.3 us (0.88)
  Pallas kernels: 41.4 us -> 38.3 us
  local copies, waits for them, and re-layouts: 3.91 us -> 1.72 us
    unnamed x6 -> x4, local copies, waits for them, and re-layouts: 3.91 us -> 1.72 us
    pallas_call x1, Pallas kernels: 38 us -> 36 us  [local(): pl.pallas_call(functools.partial(gather_kernel, R, C, tau_count), out_sha...]
    pallas_call x1, Pallas kernels: 3.37 us -> 2.37 us  [local(): pl.pallas_call(functools.partial(project_kernel, R, tau_count, ichunk), o...]
where the time goes in v2:
time: 40.3 us; the launch traced here: 40.1 us
  Pallas kernels  38.3 us (95%)
  local copies, waits for them, and re-layouts  1.72 us (4%)
    pallas_call x1, Pallas kernels, local(): pl.pallas_call(functools.partial(gather_kernel, R, C, tau_count), out_sha...  36 us
    pallas_call x1, Pallas kernels, local(): pl.pallas_call(functools.partial(project_kernel, R, tau_count, ichunk), o...  2.37 us
    unnamed x4, local copies, waits for them, and re-layouts  1.72 us

profile of v2, /device:TPU:0, one launch (start us, length us, event | category | flops | bytes accessed | tf_op | source)
XLA Modules:
  0.0 40.1 jit_solution(14589587356686702785)
XLA Ops:
  0.0 0.0 copy-start
  0.0 1.0 %copy-done = bf16[72,2048]{1,0:T(8,128)(2,1)S(1)} copy-done((bf16[72,2048]{1,0:T(8,128)(2,1)S(1)}, bf16[72,2048]{1,0:T(8,128)(2,1)}, u32[]{:S(2)}) %copy-start) | copy-done | bytes 294936
  1.0 0.0 copy-start.1
  1.0 0.8 %copy-done.1 = f32[4,2048]{1,0:T(4,128)S(1)} copy-done((f32[4,2048]{1,0:T(4,128)S(1)}, f32[4,2048]{1,0:T(4,128)}, u32[]{:S(2)}) %copy-start.1) | copy-done | bytes 32792
  1.7 36.0 %gather_half.1 = (bf16[4,4,144,256]{3,2,1,0:T(8,128)(2,1)S(1)}, bf16[512,288]{1,0:T(8,128)(2,1)S(1)}) custom-call(bf16[72,2048]{1,0:T(8,128)(2,1)S(1)} %copy-done, f32[4,2048]{1,0:T(4,128)S(1)} %copy-done.1, bf16[16,72,2048]{2,1,0:T(8,128)(2,1)} %w_hbm.1, bf16[1024,2048]{1,0:T(8,128)(2,1)} %xc_hbm.1), custom_call_target="tpu_custom_call" | custom-call | tf_op jit(solution)/shard_map/gather_half/pallas_call | solution.py:372
  37.7 2.4 %project.1 = f32[4,512,512]{2,1,0:T(8,128)} custom-call(bf16[4,4,144,256]{3,2,1,0:T(8,128)(2,1)S(1)} %get-tuple-element.7.hp, bf16[512,288]{1,0:T(8,128)(2,1)S(1)} %get-tuple-element.8.rbt), custom_call_target="tpu_custom_call" | custom-call | tf_op jit(solution)/shard_map/project/pallas_call | solution.py:414
Async XLA Ops:
  0.0 1.0 %copy-start = (bf16[72,2048]{1,0:T(8,128)(2,1)S(1)}, bf16[72,2048]{1,0:T(8,128)(2,1)}, u32[]{:S(2)}) copy-start(bf16[72,2048]{1,0:T(8,128)(2,1)} %xr_hbm.1) | copy-start | bytes 884740
  1.0 0.8 %copy-start.1 = (f32[4,2048]{1,0:T(4,128)S(1)}, f32[4,2048]{1,0:T(4,128)}, u32[]{:S(2)}) copy-start(f32[4,2048]{1,0:T(4,128)} %occ_hbm.1) | copy-start | bytes 98308

commit v3 on v2

--- a/solution.py
+++ b/solution.py
@@ -14,6 +14,7 @@
 CHUNK = 256
 QBLOCK = 256
 WPARTS = 2
+AHEAD = 1
 GATHER_VMEM = 52 * 1024 * 1024
 PROJECT_VMEM = 40 * 1024 * 1024
 
@@ -292,13 +293,19 @@
             weigh((k + 1) // parts)
         if k >= 2:
             finish(k - 2)
+        if k >= 2 + AHEAD and R > 1:
+            forward(1, k - 2 - AHEAD)
         if k == 2:
             basis_gathered()
     if n < 2:
         basis_gathered()
     basis_done()
 
-    @pl.loop(1, R)
+    for k in range(max(n - AHEAD, 0), n):
+        if R > 1:
+            forward(1, k)
+
+    @pl.loop(2, R)
     def _(d):
         for k in range(n):
             forward(d, k)

time: 40.3 us -> 39.5 us (0.980)
  Pallas kernels: 38.3 us -> 37.5 us
    pallas_call x1, Pallas kernels: 36 us -> 35.2 us  [local(): pl.pallas_call(functools.partial(gather_kernel, R, C, tau_count), out_sha...]
where the time goes in v3:
time: 39.5 us; the launch traced here: 39.3 us
  Pallas kernels  37.5 us (95%)
  local copies, waits for them, and re-layouts  1.72 us (4%)
    pallas_call x1, Pallas kernels, local(): pl.pallas_call(functools.partial(gather_kernel, R, C, tau_count), out_sha...  35.2 us
    pallas_call x1, Pallas kernels, local(): pl.pallas_call(functools.partial(project_kernel, R, tau_count, ichunk), o...  2.37 us
    unnamed x4, local copies, waits for them, and re-layouts  1.72 us

profile of v3, /device:TPU:0, one launch (start us, length us, event | category | flops | bytes accessed | tf_op | source)
XLA Modules:
  0.0 39.3 jit_solution(3488887774800560265)
XLA Ops:
  0.0 0.0 copy-start
  0.0 1.0 %copy-done = bf16[72,2048]{1,0:T(8,128)(2,1)S(1)} copy-done((bf16[72,2048]{1,0:T(8,128)(2,1)S(1)}, bf16[72,2048]{1,0:T(8,128)(2,1)}, u32[]{:S(2)}) %copy-start) | copy-done | bytes 294936
  1.0 0.0 copy-start.1
  1.0 0.8 %copy-done.1 = f32[4,2048]{1,0:T(4,128)S(1)} copy-done((f32[4,2048]{1,0:T(4,128)S(1)}, f32[4,2048]{1,0:T(4,128)}, u32[]{:S(2)}) %copy-start.1) | copy-done | bytes 32792
  1.7 35.2 %gather_half.1 = (bf16[4,4,144,256]{3,2,1,0:T(8,128)(2,1)S(1)}, bf16[512,288]{1,0:T(8,128)(2,1)S(1)}) custom-call(bf16[72,2048]{1,0:T(8,128)(2,1)S(1)} %copy-done, f32[4,2048]{1,0:T(4,128)S(1)} %copy-done.1, bf16[16,72,2048]{2,1,0:T(8,128)(2,1)} %w_hbm.1, bf16[1024,2048]{1,0:T(8,128)(2,1)} %xc_hbm.1), custom_call_target="tpu_custom_call" | custom-call | tf_op jit(solution)/shard_map/gather_half/pallas_call | solution.py:379
  36.9 2.4 %project.1 = f32[4,512,512]{2,1,0:T(8,128)} custom-call(bf16[4,4,144,256]{3,2,1,0:T(8,128)(2,1)S(1)} %get-tuple-element.7.hp, bf16[512,288]{1,0:T(8,128)(2,1)S(1)} %get-tuple-element.8.rbt), custom_call_target="tpu_custom_call" | custom-call | tf_op jit(solution)/shard_map/project/pallas_call | solution.py:421
Async XLA Ops:
  0.0 1.0 %copy-start = (bf16[72,2048]{1,0:T(8,128)(2,1)S(1)}, bf16[72,2048]{1,0:T(8,128)(2,1)}, u32[]{:S(2)}) copy-start(bf16[72,2048]{1,0:T(8,128)(2,1)} %xr_hbm.1) | copy-start | bytes 884740
  1.0 0.8 %copy-start.1 = (f32[4,2048]{1,0:T(4,128)S(1)}, f32[4,2048]{1,0:T(4,128)}, u32[]{:S(2)}) copy-start(f32[4,2048]{1,0:T(4,128)} %occ_hbm.1) | copy-start | bytes 98308
